TPU v7x, 512 devices: a whole 4x4x16 slice. The times are simulated.
512 devices in a mesh: tm: 32 (over y, x, core), stream: 16 (over z).
Axes of the slice: x: 4, y: 4, z: 16, core: 2. Of those that a mesh axis runs over, the one named last changes fastest.
Arguments:
- tokens: bfloat16 [65536, 2048], P(('tm', 'stream')), may hold values from -6 to 6
- w_query: bfloat16 [2048, 2048], P('stream'), may hold values from -0.125 to 0.125
- w_key: bfloat16 [2048, 2048], P('stream'), may hold values from -0.125 to 0.125
- w_value: bfloat16 [2048, 2048], P('stream'), may hold values from -0.125 to 0.125
- decay_proj: bfloat16 [2048, 16], P('stream'), may hold values from -0.125 to 0.125
- beta_proj: bfloat16 [2048, 16], P('stream'), may hold values from -0.125 to 0.125
- decay_rate: float32 [16], replicated, may hold values from 1.5258789e-05 to 0.1
- beta_bias: float32 [16], replicated, may hold values from -7 to 0
- norm_gain: float32 [128], replicated, may hold values from 0.5 to 1.5
Outputs:
- mixed: bfloat16 [65536, 2048], P(('tm', 'stream'))
All inputs are finite; a program needn't handle non-finite values.
Results may differ from a plain program's by a relative error of at most 0.0073.
Values may be sent and summed in bfloat16 or wider, within the bound.
No kernel may reach another device: no remote copies, remote signals or barrier semaphores. Data moves between devices by JAX's collectives and lax.ppermute only.
A program may use at most 128 MiB of HBM per device.

v0:
```python
import jax
import jax.numpy as jnp
from jax import lax
from jax.sharding import Mesh
from jax.sharding import PartitionSpec as P

HEADS = 16
DK = 128
DV = 128
GROUP = 256
TM = ("tm_0", "tm_1", "tm_2")
TM_STREAM = ("tm_0", "tm_1", "tm_2", "stream")
highest_precision = lax.Precision.HIGHEST


def in_one_piece(arrays, axis, dim, along):
    widths = [a.shape[along] for a in arrays]
    both = jnp.concatenate(arrays, axis=along)
    whole = lax.all_gather(both, axis, axis=dim, tiled=True)
    return tuple(jnp.split(whole, [sum(widths[:k]) for k in range(1, len(widths))], axis=along))


def nothing_yet(x, identity):
    return jax.tree.map(
        lambda a, e: jnp.broadcast_to(jnp.asarray(e, a.dtype), a.shape), x, identity
    )


def carried_in(x, axes, combine, identity):
    before = start = nothing_yet(x, identity)
    subtotal = x
    for axis in reversed(axes):
        length, place = (lax.axis_size(axis), lax.axis_index(axis))
        pieces = jax.tree.map(lambda part: lax.all_gather(part, axis), subtotal)
        inside, subtotal = (start, start)
        for k in range(length):
            passed = k < place
            subtotal = combine(subtotal, jax.tree.map(lambda part: part[k], pieces))
            inside = jax.tree.map(lambda new, old: jnp.where(passed, new, old), subtotal, inside)
        before = combine(inside, before)
    return before


def add_rows(inputs, piece):
    return jnp.dot(inputs, piece, preferred_element_type=jnp.float32)


def compose_pairs(earlier, later):
    first_map, first_shift = earlier
    second_map, second_shift = later
    joined_map = jnp.einsum("udf,ufe->ude", first_map, second_map, precision=highest_precision)
    joined_shift = (
        jnp.einsum("ued,udf->uef", first_shift, second_map, precision=highest_precision)
        + second_shift
    )
    return (joined_map, joined_shift)


def shards(
    tokens, w_query, w_key, w_value, decay_proj, beta_proj, decay_rate, beta_bias, norm_gain
):
    local_rows = tokens.shape[0]
    streams = lax.axis_size("stream")
    per_device = HEADS // streams

    def fold_one(piece):
        return add_rows(tokens, piece)

    raw_query = fold_one(lax.all_gather(w_query, "stream", axis=0, tiled=True))
    raw_key = fold_one(lax.all_gather(w_key, "stream", axis=0, tiled=True))
    raw_value = fold_one(lax.all_gather(w_value, "stream", axis=0, tiled=True))
    pieces = in_one_piece((decay_proj, beta_proj), "stream", 0, 1)
    decay_logit, beta_logit = tuple((add_rows(tokens, piece) for piece in pieces))
    query_heads = raw_query.reshape(local_rows, HEADS, DK)
    key_heads = raw_key.reshape(local_rows, HEADS, DK)
    queries = (
        (
            query_heads
            * lax.rsqrt(jnp.sum(query_heads * query_heads, -1, keepdims=True) + 1e-06)
            * DK ** (-0.5)
        )
        .astype(jnp.bfloat16)
        .reshape(local_rows, HEADS * DK)
    )
    key_rows = (
        (key_heads * lax.rsqrt(jnp.sum(key_heads * key_heads, -1, keepdims=True) + 1e-06))
        .astype(jnp.bfloat16)
        .reshape(local_rows, HEADS * DK)
    )
    values = raw_value.astype(jnp.bfloat16)
    log_decay = (-decay_rate * jax.nn.softplus(decay_logit)).astype(jnp.bfloat16)
    strength = jax.nn.sigmoid(beta_logit + beta_bias).astype(jnp.bfloat16)
    got_query, got_key, got_value, got_decay, got_strength = (
        lax.all_to_all(queries, "stream", split_axis=1, concat_axis=0, tiled=True),
        lax.all_to_all(key_rows, "stream", split_axis=1, concat_axis=0, tiled=True),
        lax.all_to_all(values, "stream", split_axis=1, concat_axis=0, tiled=True),
        lax.all_to_all(log_decay, "stream", split_axis=1, concat_axis=0, tiled=True),
        lax.all_to_all(strength, "stream", split_axis=1, concat_axis=0, tiled=True),
    )
    block_rows = got_query.shape[0]
    num_blocks = block_rows // GROUP
    query_b = (
        got_query.reshape(num_blocks, GROUP, per_device, DK)
        .astype(jnp.float32)
        .transpose(0, 2, 1, 3)
    )
    key_b = (
        got_key.reshape(num_blocks, GROUP, per_device, DK).astype(jnp.float32).transpose(0, 2, 1, 3)
    )
    value_b = (
        got_value.reshape(num_blocks, GROUP, per_device, DV)
        .astype(jnp.float32)
        .transpose(0, 2, 1, 3)
    )
    decay_b = (
        got_decay.reshape(num_blocks, GROUP, per_device).astype(jnp.float32).transpose(0, 2, 1)
    )
    strength_b = (
        got_strength.reshape(num_blocks, GROUP, per_device).astype(jnp.float32).transpose(0, 2, 1)
    )
    positions = jnp.arange(GROUP)
    strict = positions[:, None] > positions[None, :]
    inclusive_mask = positions[:, None] >= positions[None, :]
    identity = jnp.eye(GROUP, dtype=jnp.float32)
    key_identity = jnp.eye(DK, dtype=jnp.float32)
    cumulative = jnp.cumsum(decay_b, axis=2)
    growth = jnp.exp(cumulative)
    last_log = cumulative[..., -1:]
    tail = jnp.exp(last_log - cumulative)
    key_products = jnp.einsum("nucd,numd->nucm", key_b, key_b, precision=highest_precision)
    spread = cumulative[..., :, None] - cumulative[..., None, :]
    decay_matrix = jnp.exp(jnp.where(inclusive_mask, spread, 0.0))
    lower = (
        jnp.where(strict, strength_b[..., :, None] * decay_matrix * key_products, 0.0) + identity
    )
    right_side = jnp.concatenate(
        [(strength_b * growth)[..., None] * key_b, strength_b[..., None] * value_b], -1
    )
    solved = jax.scipy.linalg.solve_triangular(lower, right_side, lower=True, unit_diagonal=True)
    weights_w = solved[..., :DK]
    updates = solved[..., DK:]
    key_tail = tail[..., None] * key_b
    attention_scores = jnp.where(
        inclusive_mask,
        jnp.einsum("nucd,numd->nucm", query_b, key_b, precision=highest_precision) * decay_matrix,
        0.0,
    )
    query_grown = growth[..., None] * query_b
    block_map = jnp.exp(last_log)[..., None] * key_identity - jnp.einsum(
        "nucd,nuce->nude", weights_w, key_tail, precision=highest_precision
    )
    block_shift = jnp.einsum("nuce,nucd->nued", updates, key_tail, precision=highest_precision)

    def compose_step(carry, pair):
        return (compose_pairs(carry, pair), carry)

    start_map = jnp.broadcast_to(key_identity, (per_device, DK, DK))
    start_shift = jnp.zeros((per_device, DV, DK), jnp.float32)
    totals, prefixes = lax.scan(compose_step, (start_map, start_shift), (block_map, block_shift))
    total_map, total_shift = totals
    prefix_map, prefix_shift = prefixes
    scanned = carried_in((total_map, total_shift), TM, compose_pairs, (start_map, start_shift))
    state_in = scanned[1]
    block_states = (
        jnp.einsum("ued,nudf->nuef", state_in, prefix_map, precision=highest_precision)
        + prefix_shift
    )
    fresh = updates - jnp.einsum(
        "nucd,nued->nuce", weights_w, block_states, precision=highest_precision
    )
    read = jnp.einsum(
        "nucd,nued->nuce", query_grown, block_states, precision=highest_precision
    ) + jnp.einsum("nucm,nume->nuce", attention_scores, fresh, precision=highest_precision)
    readout = read.transpose(0, 2, 1, 3).reshape(block_rows, per_device * DV).astype(jnp.bfloat16)
    returned = lax.all_to_all(readout, "stream", split_axis=0, concat_axis=1, tiled=True)
    head_read = returned.reshape(local_rows, HEADS, DV).astype(jnp.float32)
    normed = (
        head_read
        * lax.rsqrt(jnp.mean(head_read * head_read, -1, keepdims=True) + 1e-06)
        * norm_gain
    )
    return normed.reshape(local_rows, HEADS * DV).astype(jnp.bfloat16)


def solution(mesh):
    finer = Mesh(
        mesh.devices.reshape(4, 4, 2, mesh.shape["stream"]), ("tm_0", "tm_1", "tm_2", "stream")
    )
    return jax.shard_map(
        shards,
        mesh=finer,
        in_specs=(
            P(TM_STREAM, None),
            P("stream", None),
            P("stream", None),
            P("stream", None),
            P("stream", None),
            P("stream", None),
            P(),
            P(),
            P(),
        ),
        out_specs=P(TM_STREAM, None),
        check_vma=False,
    )
```

profile of v0, /device:TPU:34, one launch (start us, length us, event | category | flops | bytes accessed | tf_op | source)
XLA Modules:
  0.0 717.1 jit_solution(13404925184703037204)
XLA Ops:
  10.1 34.2 %all_gather.48 = bf16[2048,32]{0,1:T(8,128)(2,1)S(1)} all-gather(bf16[128,32]{0,1:T(8,128)(2,1)S(1)} %pad_maximum_fusion), channel_id=1, replica_groups=mesh['tm_0'=4,'tm_1'=4,'tm_2'=2,'stream'=16] {'stream'}, dimensions={0}, use_global_device_ids=true | all-gather | bytes 139264 | tf_op jit(solution)/shard_map/all_gather | solution.py:19
  45.2 9.1 %all-to-all-start = ((bf16[128,16,1]{0,2,1:T(2,128)(2,1)}), bf16[128,16,1]{0,2,1:T(2,128)(2,1)S(1)}, u32[]{:S(2)}, u32[]{:S(2)}) async-start(bf16[128,16,1]{0,2,1:T(2,128)(2,1)} %copy.65), calls=%async_computation | async-start | bytes 16384 | tf_op jit(solution)/shard_map/all_to_all | solution.py:97
  56.8 8.6 %all-to-all-done = bf16[128,16,1]{0,2,1:T(2,128)(2,1)S(1)} async-done(((bf16[128,16,1]{0,2,1:T(2,128)(2,1)}), bf16[128,16,1]{0,2,1:T(2,128)(2,1)S(1)}, u32[]{:S(2)}, u32[]{:S(2)}) %all-to-all-start) | async-done | bytes 4128 | tf_op jit(solution)/shard_map/all_to_all | solution.py:97
  65.4 4.6 all-to-all-start.2
  70.8 47.6 %all-gather.14.cloned.1.call-done = bf16[2048,2048]{1,0:T(8,128)(2,1)} async-done(((bf16[128,2048]{1,0:T(8,128)(2,1)}), bf16[2048,2048]{1,0:T(8,128)(2,1)}) %all-gather.14.cloned.1.call-update) | async-done | bytes 8388624 | tf_op jit(solution)/shard_map/all_gather | solution.py:71
  118.4 4.6 fusion.21
  124.0 11.4 %all-to-all-start.4 = ((bf16[128,16,128]{2,0,1:T(8,128)(2,1)}), bf16[128,16,128]{2,0,1:T(8,128)(2,1)S(1)}, u32[]{:S(2)}, u32[]{:S(2)}) async-start(bf16[128,16,128]{2,0,1:T(8,128)(2,1)} %bitcast.256), calls=%async_computation.4 | async-start | bytes 1048576 | tf_op jit(solution)/shard_map/all_to_all | solution.py:96
  135.6 109.5 %all-gather.12.cloned.1.call-done = bf16[2048,2048]{1,0:T(8,128)(2,1)} async-done(((bf16[128,2048]{1,0:T(8,128)(2,1)}), bf16[2048,2048]{1,0:T(8,128)(2,1)}) %all-gather.12.cloned.1.call-update) | async-done | bytes 8388624 | tf_op jit(solution)/shard_map/all_gather | solution.py:70
  245.0 4.6 fusion.143
  250.7 1.2 copy_bitcast_fusion.1
  251.9 11.1 %all-to-all-start.3 = ((bf16[128,16,128]{2,0,1:T(8,128)(2,1)}), bf16[128,16,128]{2,0,1:T(8,128)(2,1)S(1)}, u32[]{:S(2)}, u32[]{:S(2)}) async-start(bf16[128,16,128]{2,0,1:T(8,128)(2,1)} %copy_bitcast_fusion.1), calls=%async_computation.3 | async-start | bytes 1048576 | tf_op jit(solution)/shard_map/all_to_all | solution.py:95
  263.3 109.3 %all-gather.10.cloned.1.call-done = bf16[2048,2048]{1,0:T(8,128)(2,1)} async-done(((bf16[128,2048]{1,0:T(8,128)(2,1)}), bf16[2048,2048]{1,0:T(8,128)(2,1)}) %all-gather.10.cloned.1.call-update) | async-done | bytes 8388624 | tf_op jit(solution)/shard_map/all_gather | solution.py:69
  372.6 4.6 fusion.142
  378.3 1.2 copy_bitcast_fusion.2
  379.6 1.3 broadcast_multiply_fusion
  380.9 11.2 %all-to-all-start.1 = ((bf16[128,16,128]{2,0,1:T(8,128)(2,1)}), bf16[128,16,128]{2,0,1:T(8,128)(2,1)}, u32[]{:S(2)}, u32[]{:S(2)}) async-start(bf16[128,16,128]{2,0,1:T(8,128)(2,1)} %copy_bitcast_fusion.2), calls=%async_computation.1 | async-start | bytes 1048576 | tf_op jit(solution)/shard_map/all_to_all | solution.py:94
  392.1 2.1 select_add_fusion
  394.3 5.6 while.18
  394.9 2.2 bitcast_dynamic-update-slice_fusion.6
  397.7 2.2 bitcast_dynamic-update-slice_fusion.6
  399.9 158.6 %custom-call.4 = f32[8,2,128,128]{2,3,1,0:T(8,128)} custom-call(f32[8,2,128,128]{3,2,1,0:T(8,128)} %bitcast.294), custom_call_target="InvertDiagBlocksLowerTriangular" | custom-call | tf_op jit(solution)/shard_map/jit(_solve_triangular)/vmap()/triangular_solve | solution.py:139
  564.4 2.9 convolution_bitcast_fusion.3
  567.4 2.9 fusion.22
  570.3 31.5 %while.17 = (s32[]{:T(128)}, f32[1,128,128]{1,2,0:T(8,128)S(1)}, f32[1,128,128]{1,2,0:T(8,128)S(1)}, f32[8,1,128,128]{2,3,1,0:T(8,128)}, f32[8,1,128,128]{2,3,1,...) while((s32[]{:T(128)}, f32[1,128,128]{1,2,0:T(8,128)S(1)}, ...), condition=%wide.region_5.6_spmd, body=%wide.region_4.5_spmd.sunk | while | flops 50348032 | bytes 1245293 | solution.py:159
  571.9 1.1 fusion.189
  573.0 1.1 convolution_bitcast_fusion.7
  575.8 1.1 fusion.189
  577.0 1.1 convolution_bitcast_fusion.7
  580.9 1.1 convolution_bitcast_fusion.7
  584.8 1.1 convolution_bitcast_fusion.7
  587.6 1.1 fusion.189
  588.7 1.1 convolution_bitcast_fusion.7
  592.6 1.1 convolution_bitcast_fusion.7
  596.6 1.1 convolution_bitcast_fusion.7
  600.5 1.1 convolution_bitcast_fusion.7
  601.9 1.9 all-gather
  605.3 12.5 %all-gather.1 = f32[512,128]{1,0:T(8,128)S(1)} all-gather(f32[128,128]{1,0:T(8,128)S(1)} %fusion.92), channel_id=3, replica_groups=mesh['tm_0'=4,'tm_1'=4,'tm_2'=2,'stream'=16] {'tm_1'}, dimensions={0}, use_global_device_ids=true | all-gather | bytes 327680 | tf_op jit(solution)/shard_map/all_gather | solution.py:34
  619.9 2.2 all-gather.3
  623.6 12.7 %all-gather.2 = f32[512,128]{1,0:T(8,128)S(1)} all-gather(f32[128,128]{1,0:T(8,128)S(1)} %fusion.98), channel_id=4, replica_groups=mesh['tm_0'=4,'tm_1'=4,'tm_2'=2,'stream'=16] {'tm_0'}, dimensions={0}, use_global_device_ids=true | all-gather | bytes 327680 | tf_op jit(solution)/shard_map/all_gather | solution.py:34
  637.4 12.3 %all-gather.4 = f32[512,128]{1,0:T(8,128)S(1)} all-gather(f32[128,128]{1,0:T(8,128)S(1)} %convolution_add_fusion.7), channel_id=6, replica_groups=mesh['tm_0'=4,'tm_1'=4,'tm_2'=2,'stream'=16] {'tm_1'}, dimensions={0}, use_global_device_ids=true | all-gather | bytes 327680 | tf_op jit(solution)/shard_map/all_gather | solution.py:34
  651.1 12.3 %all-gather.5 = f32[512,128]{1,0:T(8,128)S(1)} all-gather(f32[128,128]{1,0:T(8,128)S(1)} %convolution_add_fusion.4), channel_id=7, replica_groups=mesh['tm_0'=4,'tm_1'=4,'tm_2'=2,'stream'=16] {'tm_0'}, dimensions={0}, use_global_device_ids=true | all-gather | bytes 327680 | tf_op jit(solution)/shard_map/all_gather | solution.py:34
  666.3 2.0 fusion.17
  668.4 1.6 fusion.145
  670.0 2.2 fusion.47
  672.2 3.3 fusion.18
  675.5 12.0 %all-to-all-start.5 = ((bf16[16,128,128]{2,1,0:T(8,128)(2,1)}), bf16[16,128,128]{2,1,0:T(8,128)(2,1)S(1)}, u32[]{:S(2)}, u32[]{:S(2)}) async-start(bf16[16,128,128]{2,1,0:T(8,128)(2,1)} %bitcast.59), calls=%async_computation.5 | async-start | bytes 1048576 | tf_op jit(solution)/shard_map/all_to_all | solution.py:175
  687.6 21.5 %all-to-all-done.5 = bf16[16,128,128]{2,1,0:T(8,128)(2,1)S(1)} async-done(((bf16[16,128,128]{2,1,0:T(8,128)(2,1)}), bf16[16,128,128]{2,1,0:T(8,128)(2,1)S(1)}, u32[]{:S(2)}, u32[]{:S(2)}) %all-to-all-start.5) | async-done | bytes 524320 | tf_op jit(solution)/shard_map/all_to_all | solution.py:175
  709.4 1.1 fusion.40
  (178 shorter events, 47.6 us)
Async XLA Ops:
  6.5 37.8 %copy-start = (bf16[128,2048]{1,0:T(8,128)(2,1)S(1)}, bf16[128,2048]{1,0:T(8,128)(2,1)}, u32[]{:S(2)}) copy-start(bf16[128,2048]{1,0:T(8,128)(2,1)} %param.11) | copy-start | bytes 1572868
  6.5 48.7 %copy-start.21 = (f32[16]{0:T(128)S(1)}, f32[16]{0:T(128)}, u32[]{:S(2)}) copy-start(f32[16]{0:T(128)} %param.18) | copy-start | bytes 196
  6.5 111.9 %all-gather.14.cloned.1.call-start = ((), (), s32[]{:S(2)}) async-start(), calls=%async_computation.8 | async-start | bytes 8912896 | tf_op jit(solution)/shard_map/all_gather | solution.py:71
  7.3 237.8 %all-gather.12.cloned.1.call-start = ((), (), s32[]{:S(2)}) async-start(), calls=%async_computation.7 | async-start | bytes 8912896 | tf_op jit(solution)/shard_map/all_gather | solution.py:70
  8.0 364.6 %all-gather.10.cloned.1.call-start = ((), (), s32[]{:S(2)}) async-start(), calls=%async_computation.6 | async-start | bytes 8912896 | tf_op jit(solution)/shard_map/all_gather | solution.py:69
  45.2 20.2 %all-to-all-start = ((bf16[128,16,1]{0,2,1:T(2,128)(2,1)}), bf16[128,16,1]{0,2,1:T(2,128)(2,1)S(1)}, u32[]{:S(2)}, u32[]{:S(2)}) async-start(bf16[128,16,1]{0,2,1:T(2,128)(2,1)} %copy.65), calls=%async_computation | async-start | bytes 16384 | tf_op jit(solution)/shard_map/all_to_all | solution.py:97
  54.3 337.8 %copy-start.15 = (pred[256,256]{1,0:T(8,128)(4,1)}, pred[256,256]{1,0:T(8,128)(4,1)S(1)}, u32[]{:S(2)}) copy-start(pred[256,256]{1,0:T(8,128)(4,1)S(1)} %iota_compare_fusion.2) | copy-start | bytes 196612
  65.4 58.6 %all-to-all-start.2 = ((bf16[128,16,1]{0,2,1:T(2,128)(2,1)}), bf16[128,16,1]{0,2,1:T(2,128)(2,1)S(1)}, u32[]{:S(2)}, u32[]{:S(2)}) async-start(bf16[128,16,1]{0,2,1:T(2,128)(2,1)} %copy.68), calls=%async_computation.2 | async-start | bytes 16384 | tf_op jit(solution)/shard_map/all_to_all | solution.py:98
  124.0 127.9 %all-to-all-start.4 = ((bf16[128,16,128]{2,0,1:T(8,128)(2,1)}), bf16[128,16,128]{2,0,1:T(8,128)(2,1)S(1)}, u32[]{:S(2)}, u32[]{:S(2)}) async-start(bf16[128,16,128]{2,0,1:T(8,128)(2,1)} %bitcast.256), calls=%async_computation.4 | async-start | bytes 1048576 | tf_op jit(solution)/shard_map/all_to_all | solution.py:96
  251.9 125.4 %copy-start.5 = (bf16[128,16,128]{2,0,1:T(8,128)(2,1)}, bf16[128,16,128]{2,0,1:T(8,128)(2,1)S(1)}, u32[]{:S(2)}) copy-start(bf16[128,16,128]{2,0,1:T(8,128)(2,1)S(1)} %all-to-all-done.4) | copy-start | bytes 1572868
  251.9 129.1 %all-to-all-start.3 = ((bf16[128,16,128]{2,0,1:T(8,128)(2,1)}), bf16[128,16,128]{2,0,1:T(8,128)(2,1)S(1)}, u32[]{:S(2)}, u32[]{:S(2)}) async-start(bf16[128,16,128]{2,0,1:T(8,128)(2,1)} %copy_bitcast_fusion.1), calls=%async_computation.3 | async-start | bytes 1048576 | tf_op jit(solution)/shard_map/all_to_all | solution.py:95
  377.9 1.6 copy-start.6
  379.5 12.6 %copy-start.17 = (pred[256,256]{1,0:T(8,128)(4,1)S(1)}, pred[256,256]{1,0:T(8,128)(4,1)}, u32[]{:S(2)}) copy-start(pred[256,256]{1,0:T(8,128)(4,1)} %get-tuple-element.118) | copy-start | bytes 196612
  380.9 287.4 %all-to-all-start.1 = ((bf16[128,16,128]{2,0,1:T(8,128)(2,1)}), bf16[128,16,128]{2,0,1:T(8,128)(2,1)}, u32[]{:S(2)}, u32[]{:S(2)}) async-start(bf16[128,16,128]{2,0,1:T(8,128)(2,1)} %copy_bitcast_fusion.2), calls=%async_computation.1 | async-start | bytes 1048576 | tf_op jit(solution)/shard_map/all_to_all | solution.py:94
  558.5 1.2 copy-start.3
  559.8 1.2 copy-start.8
  603.8 0.8 copy-start.7
  604.6 0.6 copy-start.10
  605.3 18.3 %copy-start.9 = (f32[128,128]{1,0:T(8,128)}, f32[128,128]{1,0:T(8,128)S(1)}, u32[]{:S(2)}) copy-start(f32[128,128]{1,0:T(8,128)S(1)} %fusion.92) | copy-start | bytes 196612
  619.9 31.0 %copy-start.11 = (f32[128,128]{1,0:T(8,128)S(1)}, f32[128,128]{1,0:T(8,128)}, u32[]{:S(2)}) copy-start(f32[128,128]{1,0:T(8,128)} %copy-done.10) | copy-start | bytes 196612
  619.9 44.2 %copy-start.12 = (f32[128,128]{1,0:T(8,128)S(1)}, f32[128,128]{1,0:T(8,128)}, u32[]{:S(2)}) copy-start(f32[128,128]{1,0:T(8,128)} %fusion.88) | copy-start | bytes 196612
  622.1 42.4 %copy-start.19 = (f32[128]{0:T(128)S(1)}, f32[128]{0:T(128)}, u32[]{:S(2)}) copy-start(f32[128]{0:T(128)} %multiply_reduce_fusion.1) | copy-start | bytes 1540
  623.4 41.3 %copy-start.18 = (f32[128]{0:T(128)S(1)}, f32[128]{0:T(128)}, u32[]{:S(2)}) copy-start(f32[128]{0:T(128)} %multiply_reduce_fusion) | copy-start | bytes 1540
  623.6 41.3 %copy-start.13 = (f32[8,1,128,128]{2,3,1,0:T(8,128)S(1)}, f32[8,1,128,128]{2,3,1,0:T(8,128)}, u32[]{:S(2)}) copy-start(f32[8,1,128,128]{2,3,1,0:T(8,128)} %get-tuple-element.48) | copy-start | bytes 1572868
  623.6 41.3 %copy-start.14 = (f32[8,1,128,128]{2,3,1,0:T(8,128)S(1)}, f32[8,1,128,128]{2,3,1,0:T(8,128)}, u32[]{:S(2)}) copy-start(f32[8,1,128,128]{2,3,1,0:T(8,128)} %get-tuple-element.45) | copy-start | bytes 1572868
  665.5 0.8 copy-start.1
  668.4 1.6 copy-start.2
  668.4 3.8 copy-start.4
  668.4 3.9 copy-start.16
  672.2 15.3 %copy-start.20 = (f32[128]{0:T(128)S(1)}, f32[128]{0:T(128)}, u32[]{:S(2)}) copy-start(f32[128]{0:T(128)} %param.19) | copy-start | bytes 1540
  675.5 33.5 %all-to-all-start.5 = ((bf16[16,128,128]{2,1,0:T(8,128)(2,1)}), bf16[16,128,128]{2,1,0:T(8,128)(2,1)S(1)}, u32[]{:S(2)}, u32[]{:S(2)}) async-start(bf16[16,128,128]{2,1,0:T(8,128)(2,1)} %bitcast.59), calls=%async_computation.5 | async-start | bytes 1048576 | tf_op jit(solution)/shard_map/all_to_all | solution.py:175
Sparse Core Ops, SparseCore 0:
  9.4 108.9 all-gather.13
  120.5 124.5 all-gather.11
  247.1 125.4 all-gather.9
where the time goes:
time: 719 us; the launch traced here: 717 us
  waiting for transfers between devices  299 us (42%)
  other arithmetic  171 us (24%)
  blocking collectives  88 us (12%)
  matrix products  59.8 us (8%)
  starting transfers between devices  59.5 us (8%)
  local copies, waits for them, and re-layouts  26.1 us (4%)
  between operations  13.7 us (2%)
    another operation x3, other arithmetic, shards(): jax.scipy.linalg.solve_triangular(lower, right_side, lower=True, unit_dia...  159 us
    all_gather x1, waiting for transfers between devices, shards(): raw_key = fold_one(lax.all_gather(w_key, 'stream', axis=0, tiled=True))  109 us
    all_gather x1, waiting for transfers between devices, shards(): raw_query = fold_one(lax.all_gather(w_query, 'stream', axis=0, tiled=True))  109 us
    all_gather x6, blocking collectives, carried_in(): pieces = jax.tree.map(lambda part: lax.all_gather(part, axis), subtotal)  53.8 us
    all_gather x1, waiting for transfers between devices, shards(): raw_value = fold_one(lax.all_gather(w_value, 'stream', axis=0, tiled=True))  47.6 us
    all_gather x1, blocking collectives, in_one_piece(): whole = lax.all_gather(both, axis, axis=dim, tiled=True)  34.2 us
    all_to_all x1, waiting for transfers between devices, shards(): lax.all_to_all(readout, 'stream', split_axis=0, concat_axis=1, tiled=True)  21.5 us
    dot_general x5, matrix products, add_rows(): return jnp.dot(inputs, piece, preferred_element_type=jnp.float32)  14.4 us
  transfers between devices with their start and end apart: 9, of which 5 were waited for; matrix products, arithmetic and copies ran while one was open for 34% of the time, Pallas kernels for 0%

commit v1 on v0

--- a/solution.py
+++ b/solution.py
@@ -11,6 +11,11 @@
 TM = ("tm_0", "tm_1", "tm_2")
 TM_STREAM = ("tm_0", "tm_1", "tm_2", "stream")
 highest_precision = lax.Precision.HIGHEST
+
+
+def gather_over(x, name, dim):
+    sent = jnp.stack([x] * lax.axis_size(name))
+    return jnp.concatenate(lax.all_to_all(sent, name, 0, 0), axis=dim)
 
 
 def in_one_piece(arrays, axis, dim, along):
@@ -68,7 +73,7 @@
 
     raw_query = fold_one(lax.all_gather(w_query, "stream", axis=0, tiled=True))
     raw_key = fold_one(lax.all_gather(w_key, "stream", axis=0, tiled=True))
-    raw_value = fold_one(lax.all_gather(w_value, "stream", axis=0, tiled=True))
+    raw_value = fold_one(gather_over(w_value, "stream", 0))
     pieces = in_one_piece((decay_proj, beta_proj), "stream", 0, 1)
     decay_logit, beta_logit = tuple((add_rows(tokens, piece) for piece in pieces))
     query_heads = raw_query.reshape(local_rows, HEADS, DK)

time: 719 us -> 1010 us (1.40)
  waiting for transfers between devices: 299 us -> 563 us
  blocking collectives: 88 us -> 120 us
    all_gather x1, waiting for transfers between devices: 109 us -> 446 us  [shards(): raw_query = fold_one(lax.all_gather(w_query, 'stream', axis=0, tiled=True))]
    all_gather x1 -> x0, waiting for transfers between devices: 47.6 us -> none  [shards(): raw_value = fold_one(lax.all_gather(w_value, 'stream', axis=0, tiled=True))]
    all_gather x1, waiting for transfers between devices: 109 us -> 63.7 us  [shards(): raw_key = fold_one(lax.all_gather(w_key, 'stream', axis=0, tiled=True))]
    all_to_all x0 -> x1, blocking collectives: none -> 31.5 us  [shards(): lax.all_to_all(key_rows, 'stream', split_axis=1, concat_axis=0, tiled=True)]
    all_to_all x1, waiting for transfers between devices: 0.01 us -> 21.2 us  [shards(): lax.all_to_all(queries, 'stream', split_axis=1, concat_axis=0, tiled=True)]
    all_to_all x1, waiting for transfers between devices: 0.01 us -> 10.3 us  [shards(): lax.all_to_all(strength, 'stream', split_axis=1, concat_axis=0, tiled=True)]
  transfers between devices with their start and end apart: 9 -> 8, of which waited for: 5 -> 5; matrix products, arithmetic and copies ran while one was open for 34% -> 19% of each run, Pallas kernels for 0% -> 0%
where the time goes in v1:
time: 1010 us
  waiting for transfers between devices  563 us (56%)
  other arithmetic  169 us (17%)
  blocking collectives  120 us (12%)
  starting transfers between devices  57 us (6%)
  matrix products  54.7 us (5%)
  local copies, waits for them, and re-layouts  27.6 us (3%)
  between operations  14.1 us (1%)
    all_gather x1, waiting for transfers between devices, shards(): raw_query = fold_one(lax.all_gather(w_query, 'stream', axis=0, tiled=True))  446 us
    another operation x3, other arithmetic, shards(): jax.scipy.linalg.solve_triangular(lower, right_side, lower=True, unit_dia...  159 us
    all_gather x1, waiting for transfers between devices, shards(): raw_key = fold_one(lax.all_gather(w_key, 'stream', axis=0, tiled=True))  63.7 us
    all_gather x6, blocking collectives, carried_in(): pieces = jax.tree.map(lambda part: lax.all_gather(part, axis), subtotal)  54 us
    all_gather x1, blocking collectives, in_one_piece(): whole = lax.all_gather(both, axis, axis=dim, tiled=True)  34.3 us
    all_to_all x1, blocking collectives, shards(): lax.all_to_all(key_rows, 'stream', split_axis=1, concat_axis=0, tiled=True)  31.5 us
    all_to_all x1, waiting for transfers between devices, shards(): lax.all_to_all(queries, 'stream', split_axis=1, concat_axis=0, tiled=True)  21.2 us
    all_to_all x1, waiting for transfers between devices, shards(): lax.all_to_all(readout, 'stream', split_axis=0, concat_axis=1, tiled=True)  20.2 us
  transfers between devices with their start and end apart: 8, of which 5 were waited for; matrix products, arithmetic and copies ran while one was open for 19% of the time, Pallas kernels for 0%

profile of v1, /device:TPU:34, one launch (start us, length us, event | category | flops | bytes accessed | tf_op | source)
XLA Modules:
  0.0 1005.4 jit_solution(14704860400169249311)
XLA Ops:
  8.6 34.3 %all_gather.45 = bf16[2048,32]{0,1:T(8,128)(2,1)S(1)} all-gather(bf16[128,32]{0,1:T(8,128)(2,1)S(1)} %pad_maximum_fusion), channel_id=1, replica_groups=mesh['tm_0'=4,'tm_1'=4,'tm_2'=2,'stream'=16] {'stream'}, dimensions={0}, use_global_device_ids=true | all-gather | bytes 139264 | tf_op jit(solution)/shard_map/all_gather | solution.py:24
  43.8 8.9 all-to-all-start
  54.1 63.7 %all-gather.11.cloned.1.call-done = bf16[2048,2048]{1,0:T(8,128)(2,1)} async-done(((bf16[128,2048]{1,0:T(8,128)(2,1)}), bf16[2048,2048]{1,0:T(8,128)(2,1)}) %all-gather.11.cloned.1.call-update) | async-done | bytes 8388624 | tf_op jit(solution)/shard_map/all_gather | solution.py:75
  117.9 4.6 fusion.143
  123.2 11.5 %all-to-all-start.2 = ((bf16[128,16,1]{0,2,1:T(2,128)(2,1)}), bf16[128,16,1]{0,2,1:T(2,128)(2,1)S(1)}, u32[]{:S(2)}, u32[]{:S(2)}) async-start(bf16[128,16,1]{0,2,1:T(2,128)(2,1)} %copy.68), calls=%async_computation.2 | async-start | bytes 16384 | tf_op jit(solution)/shard_map/all_to_all | solution.py:103
  135.4 10.3 %all-to-all-done.2 = bf16[128,16,1]{0,2,1:T(2,128)(2,1)S(1)} async-done(((bf16[128,16,1]{0,2,1:T(2,128)(2,1)}), bf16[128,16,1]{0,2,1:T(2,128)(2,1)S(1)}, u32[]{:S(2)}, u32[]{:S(2)}) %all-to-all-start.2) | async-done | bytes 4128 | tf_op jit(solution)/shard_map/all_to_all | solution.py:103
  145.8 31.5 %all_to_all.86 = bf16[128,16,128]{2,0,1:T(8,128)(2,1)S(1)} all-to-all(bf16[128,16,128]{2,0,1:T(8,128)(2,1)S(1)} %copy_bitcast_fusion.1), channel_id=1, replica_groups=mesh['tm_0'=4,'tm_1'=4,'tm_2'=2,'stream'=16] {'stream'}, dimensions={1} | all-to-all | bytes 1048576 | tf_op jit(solution)/shard_map/all_to_all | solution.py:100
  177.2 4.3 stack.2
  181.5 6.7 all-to-all-start.4
  189.0 445.6 %all-gather.9.cloned.1.call-done = bf16[2048,2048]{1,0:T(8,128)(2,1)} async-done(((bf16[128,2048]{1,0:T(8,128)(2,1)}), bf16[2048,2048]{1,0:T(8,128)(2,1)}) %all-gather.9.cloned.1.call-update) | async-done | bytes 8388624 | tf_op jit(solution)/shard_map/all_gather | solution.py:74
  634.7 4.6 fusion.142
  640.3 1.2 copy_bitcast_fusion.2
  641.5 11.0 %all-to-all-start.1 = ((bf16[128,16,128]{2,0,1:T(8,128)(2,1)}), bf16[128,16,128]{2,0,1:T(8,128)(2,1)S(1)}, u32[]{:S(2)}, u32[]{:S(2)}) async-start(bf16[128,16,128]{2,0,1:T(8,128)(2,1)} %copy_bitcast_fusion.2), calls=%async_computation.1 | async-start | bytes 1048576 | tf_op jit(solution)/shard_map/all_to_all | solution.py:99
  654.5 4.7 fusion.21
  660.1 21.2 %all-to-all-done.1 = bf16[128,16,128]{2,0,1:T(8,128)(2,1)S(1)} async-done(((bf16[128,16,128]{2,0,1:T(8,128)(2,1)}), bf16[128,16,128]{2,0,1:T(8,128)(2,1)S(1)}, u32[]{:S(2)}, u32[]{:S(2)}) %all-to-all-start.1) | async-done | bytes 524320 | tf_op jit(solution)/shard_map/all_to_all | solution.py:99
  681.3 6.8 all-to-all-start.5
  689.6 5.6 while.18
  690.2 2.2 bitcast_dynamic-update-slice_fusion.6
  693.0 2.2 bitcast_dynamic-update-slice_fusion.6
  695.2 158.6 %custom-call.4 = f32[8,2,128,128]{2,3,1,0:T(8,128)} custom-call(f32[8,2,128,128]{3,2,1,0:T(8,128)} %bitcast.297), custom_call_target="InvertDiagBlocksLowerTriangular" | custom-call | tf_op jit(solution)/shard_map/jit(_solve_triangular)/vmap()/triangular_solve | solution.py:144
  853.9 1.3 convert_multiply_fusion.1
  855.2 1.8 fusion.145
  857.0 1.2 convert_element_type.187
  863.2 2.9 convolution_bitcast_fusion.3
  866.2 2.9 fusion.22
  869.1 31.3 %while.17 = (s32[]{:T(128)}, f32[1,128,128]{1,2,0:T(8,128)S(1)}, f32[1,128,128]{1,2,0:T(8,128)S(1)}, f32[8,1,128,128]{2,3,1,0:T(8,128)}, f32[8,1,128,128]{2,3,1,...) while((s32[]{:T(128)}, f32[1,128,128]{1,2,0:T(8,128)S(1)}, ...), condition=%wide.region_5.6_spmd, body=%wide.region_4.5_spmd.sunk | while | flops 50348032 | bytes 1246809 | solution.py:164
  870.7 1.1 fusion.189
  871.8 1.1 convolution_bitcast_fusion.7
  874.6 1.1 fusion.189
  875.8 1.1 convolution_bitcast_fusion.7
  878.5 1.1 fusion.189
  882.5 1.1 fusion.189
  883.6 1.1 convolution_bitcast_fusion.7
  886.4 1.1 fusion.189
  890.3 1.1 fusion.189
  894.2 1.1 fusion.189
  898.1 1.1 fusion.189
  900.5 1.9 all-gather
  902.8 12.5 %all-gather.1 = f32[512,128]{1,0:T(8,128)S(1)} all-gather(f32[128,128]{1,0:T(8,128)S(1)} %fusion.92), channel_id=3, replica_groups=mesh['tm_0'=4,'tm_1'=4,'tm_2'=2,'stream'=16] {'tm_1'}, dimensions={0}, use_global_device_ids=true | all-gather | bytes 327680 | tf_op jit(solution)/shard_map/all_gather | solution.py:39
  915.7 1.9 all-gather.3
  917.8 12.3 %all-gather.4 = f32[512,128]{1,0:T(8,128)S(1)} all-gather(f32[128,128]{1,0:T(8,128)S(1)} %convolution_add_fusion.7), channel_id=6, replica_groups=mesh['tm_0'=4,'tm_1'=4,'tm_2'=2,'stream'=16] {'tm_1'}, dimensions={0}, use_global_device_ids=true | all-gather | bytes 327680 | tf_op jit(solution)/shard_map/all_gather | solution.py:39
  931.4 12.9 %all-gather.2 = f32[512,128]{1,0:T(8,128)S(1)} all-gather(f32[128,128]{1,0:T(8,128)S(1)} %fusion.98), channel_id=4, replica_groups=mesh['tm_0'=4,'tm_1'=4,'tm_2'=2,'stream'=16] {'tm_0'}, dimensions={0}, use_global_device_ids=true | all-gather | bytes 327680 | tf_op jit(solution)/shard_map/all_gather | solution.py:39
  944.9 12.5 %all-gather.5 = f32[512,128]{1,0:T(8,128)S(1)} all-gather(f32[128,128]{1,0:T(8,128)S(1)} %convolution_add_fusion.4), channel_id=7, replica_groups=mesh['tm_0'=4,'tm_1'=4,'tm_2'=2,'stream'=16] {'tm_0'}, dimensions={0}, use_global_device_ids=true | all-gather | bytes 327680 | tf_op jit(solution)/shard_map/all_gather | solution.py:39
  960.2 1.2 fusion.47
  961.5 3.3 fusion.18
  964.8 12.0 %all-to-all-start.6 = ((bf16[16,128,128]{2,1,0:T(8,128)(2,1)}), bf16[16,128,128]{2,1,0:T(8,128)(2,1)S(1)}, u32[]{:S(2)}, u32[]{:S(2)}) async-start(bf16[16,128,128]{2,1,0:T(8,128)(2,1)} %bitcast.60), calls=%async_computation.6 | async-start | bytes 1048576 | tf_op jit(solution)/shard_map/all_to_all | solution.py:180
  976.8 20.2 %all-to-all-done.6 = bf16[16,128,128]{2,1,0:T(8,128)(2,1)S(1)} async-done(((bf16[16,128,128]{2,1,0:T(8,128)(2,1)}), bf16[16,128,128]{2,1,0:T(8,128)(2,1)S(1)}, u32[]{:S(2)}, u32[]{:S(2)}) %all-to-all-start.6) | async-done | bytes 524320 | tf_op jit(solution)/shard_map/all_to_all | solution.py:180
  997.4 1.1 fusion.40
  (161 shorter events, 42.4 us)
Async XLA Ops:
  6.5 36.3 %copy-start = (bf16[128,2048]{1,0:T(8,128)(2,1)S(1)}, bf16[128,2048]{1,0:T(8,128)(2,1)}, u32[]{:S(2)}) copy-start(bf16[128,2048]{1,0:T(8,128)(2,1)} %param.11) | copy-start | bytes 1572868
  6.5 111.3 %all-gather.11.cloned.1.call-start = ((), (), s32[]{:S(2)}) async-start(), calls=%async_computation.8 | async-start | bytes 8912896 | tf_op jit(solution)/shard_map/all_gather | solution.py:75
  43.8 79.4 %all-to-all-start = ((bf16[128,16,1]{0,2,1:T(2,128)(2,1)}), bf16[128,16,1]{0,2,1:T(2,128)(2,1)S(1)}, u32[]{:S(2)}, u32[]{:S(2)}) async-start(bf16[128,16,1]{0,2,1:T(2,128)(2,1)} %copy.65), calls=%async_computation | async-start | bytes 16384 | tf_op jit(solution)/shard_map/all_to_all | solution.py:102
  123.2 22.6 %all-to-all-start.2 = ((bf16[128,16,1]{0,2,1:T(2,128)(2,1)}), bf16[128,16,1]{0,2,1:T(2,128)(2,1)S(1)}, u32[]{:S(2)}, u32[]{:S(2)}) async-start(bf16[128,16,1]{0,2,1:T(2,128)(2,1)} %copy.68), calls=%async_computation.2 | async-start | bytes 16384 | tf_op jit(solution)/shard_map/all_to_all | solution.py:103
  135.0 42.2 %copy-start.8 = (bf16[128,2048]{1,0:T(8,128)(2,1)S(1)}, bf16[128,2048]{1,0:T(8,128)(2,1)}, u32[]{:S(2)}) copy-start(bf16[128,2048]{1,0:T(8,128)(2,1)} %param.14) | copy-start | bytes 1572868
  181.5 460.0 %all-to-all-start.4 = ((bf16[16,128,2048]{2,1,0:T(8,128)(2,1)}), bf16[16,128,2048]{2,1,0:T(8,128)(2,1)}, u32[]{:S(2)}, u32[]{:S(2)}) async-start(bf16[16,128,2048]{2,1,0:T(8,128)(2,1)} %stack.2), calls=%async_computation.4 | async-start | bytes 16777216 | tf_op jit(solution)/shard_map/all_to_all | solution.py:18
  188.2 446.4 %all-gather.9.cloned.1.call-start = ((), (), s32[]{:S(2)}) async-start(), calls=%async_computation.7 | async-start | bytes 8912896 | tf_op jit(solution)/shard_map/all_gather | solution.py:74
  641.5 39.8 %all-to-all-start.1 = ((bf16[128,16,128]{2,0,1:T(8,128)(2,1)}), bf16[128,16,128]{2,0,1:T(8,128)(2,1)S(1)}, u32[]{:S(2)}, u32[]{:S(2)}) async-start(bf16[128,16,128]{2,0,1:T(8,128)(2,1)} %copy_bitcast_fusion.2), calls=%async_computation.1 | async-start | bytes 1048576 | tf_op jit(solution)/shard_map/all_to_all | solution.py:99
  659.1 29.3 %copy-start.11 = (f32[256,256]{1,0:T(8,128)S(1)}, f32[256,256]{1,0:T(8,128)}, u32[]{:S(2)}) copy-start(f32[256,256]{1,0:T(8,128)} %get-tuple-element.119) | copy-start | bytes 786436
  659.1 29.3 %copy-start.12 = (f32[256,256]{1,0:T(8,128)S(1)}, f32[256,256]{1,0:T(8,128)}, u32[]{:S(2)}) copy-start(f32[256,256]{1,0:T(8,128)} %get-tuple-element.120) | copy-start | bytes 786436
  681.3 7.1 copy-start.3
  681.3 175.7 %all-to-all-start.5 = ((bf16[128,16,128]{2,0,1:T(8,128)(2,1)}), bf16[128,16,128]{2,0,1:T(8,128)(2,1)}, u32[]{:S(2)}, u32[]{:S(2)}) async-start(bf16[128,16,128]{2,0,1:T(8,128)(2,1)} %bitcast.257), calls=%async_computation.5 | async-start | bytes 1048576 | tf_op jit(solution)/shard_map/all_to_all | solution.py:101
  689.6 165.6 %copy-start.4 = (bf16[128,16,128]{2,0,1:T(8,128)(2,1)S(1)}, bf16[128,16,128]{2,0,1:T(8,128)(2,1)}, u32[]{:S(2)}) copy-start(bf16[128,16,128]{2,0,1:T(8,128)(2,1)} %copy-done.3) | copy-start | bytes 1572868
  857.0 1.6 copy-start.6
  858.5 1.2 copy-start.7
  930.3 28.2 %copy-start.9 = (f32[8,1,128,128]{2,3,1,0:T(8,128)S(1)}, f32[8,1,128,128]{2,3,1,0:T(8,128)}, u32[]{:S(2)}) copy-start(f32[8,1,128,128]{2,3,1,0:T(8,128)} %get-tuple-element.45) | copy-start | bytes 1572868
  930.3 28.2 %copy-start.10 = (f32[8,1,128,128]{2,3,1,0:T(8,128)S(1)}, f32[8,1,128,128]{2,3,1,0:T(8,128)}, u32[]{:S(2)}) copy-start(f32[8,1,128,128]{2,3,1,0:T(8,128)} %get-tuple-element.48) | copy-start | bytes 1572868
  958.5 1.7 copy-start.5
  959.1 2.3 copy-start.2
  961.4 15.4 %copy-start.13 = (f32[128]{0:T(128)S(1)}, f32[128]{0:T(128)}, u32[]{:S(2)}) copy-start(f32[128]{0:T(128)} %param.19) | copy-start | bytes 1540
  961.5 37.1 %copy-start.1 = (bf16[128,2048]{1,0:T(8,128)(2,1)S(1)}, bf16[128,2048]{1,0:T(8,128)(2,1)}, u32[]{:S(2)}) copy-start(bf16[128,2048]{1,0:T(8,128)(2,1)} %param.11) | copy-start | bytes 1572868
  964.8 32.3 %all-to-all-start.6 = ((bf16[16,128,128]{2,1,0:T(8,128)(2,1)}), bf16[16,128,128]{2,1,0:T(8,128)(2,1)S(1)}, u32[]{:S(2)}, u32[]{:S(2)}) async-start(bf16[16,128,128]{2,1,0:T(8,128)(2,1)} %bitcast.60), calls=%async_computation.6 | async-start | bytes 1048576 | tf_op jit(solution)/shard_map/all_to_all | solution.py:180
Sparse Core Ops, SparseCore 0:
  9.4 108.3 all-gather.10
  191.1 443.4 all-gather.8
